TPU v7x, 32 devices: a whole 2x2x4 slice. The times are simulated.
32 devices in a mesh: scen: 4 (over x, core), col: 8 (over z, y).
Axes of the slice: x: 2, y: 2, z: 4, core: 2. Of those that a mesh axis runs over, the one named last changes fastest.
Arguments:
- coupling: float32 [4, 512, 16384], P('scen', None, 'col'), may hold values from -0.25 to 0.25
- inverse_slabs: float32 [4, 512, 512], P('scen', 'col'), as said below
- barrier_diagonal: float32 [16384], replicated, may hold values from 1 to 16
Outputs:
- panel_factor: float32 [16384, 256], P('col')
Inputs may be any that keep to these rules, and one draw needn't show every extreme that they name: `inverse_slabs`: each slab is symmetric positive definite.
All inputs are finite; a program needn't handle non-finite values.
Results may differ from a plain program's by a relative error of at most 0.0001.
Values sent between devices are 32-bit elements; how exact they have to be, the bound alone decides.
A program may use at most 64 MiB of HBM per device.

v0:
```python
import jax
import jax.numpy as jnp
from jax import lax
from jax.sharding import PartitionSpec as P

PANEL = 256


def spread(value, axis, source):
    kept = jnp.where(lax.axis_index(axis) == source, value, 0).astype(value.dtype)
    return lax.psum(kept, axis)


def shards(coupling, inverse_slabs, barrier_diagonal):
    local_cols = coupling.shape[2]
    col_index = lax.axis_index("col")
    highest = lax.Precision.HIGHEST
    panel_block = spread(coupling[:, :, :PANEL], "col", 0)
    own_rows = jnp.einsum(
        "skj,sjp->skp",
        inverse_slabs,
        panel_block,
        precision=highest,
        preferred_element_type=jnp.float32,
    )
    block_piece = lax.all_gather(own_rows, "col", axis=1, tiled=True)
    running = jnp.einsum(
        "skc,skp->cp", coupling, block_piece, precision=highest, preferred_element_type=jnp.float32
    )
    pivot_run = jnp.einsum(
        "skc,skp->cp",
        panel_block,
        block_piece,
        precision=highest,
        preferred_element_type=jnp.float32,
    )
    global_rows = col_index * local_cols + jnp.arange(local_cols, dtype=jnp.int32)
    panel_ids = jnp.arange(PANEL, dtype=jnp.int32)
    diag_here = lax.dynamic_slice_in_dim(barrier_diagonal, col_index * local_cols, local_cols)
    summed, pivot_sum = lax.psum((running, pivot_run), "scen")
    pivot_matrix = pivot_sum + jnp.diag(barrier_diagonal[:PANEL])
    schur_rows = summed + jnp.where(
        global_rows[:, None] == panel_ids[None, :], diag_here[:, None], jnp.zeros_like(summed)
    )
    pivot_matrix = 0.5 * (pivot_matrix + pivot_matrix.T)
    factor = jnp.linalg.cholesky(pivot_matrix)
    solved_rows = jax.scipy.linalg.solve_triangular(factor, schur_rows.T, lower=True).T
    padded_factor = jnp.concatenate(
        [factor, jnp.zeros((local_cols - PANEL, PANEL), factor.dtype)], axis=0
    )
    return jnp.where(global_rows[:, None] < PANEL, padded_factor, solved_rows)


def solution(mesh):
    return jax.shard_map(
        shards,
        mesh=mesh,
        in_specs=(P("scen", None, "col"), P("scen", "col", None), P()),
        out_specs=P("col", None),
        check_vma=False,
    )
```

profile of v0, /device:TPU:0, one launch (start us, length us, event | category | flops | bytes accessed | tf_op | source)
XLA Modules:
  0.0 258.0 jit_solution(8957658524968874539)
XLA Ops:
  6.5 1.9 select_bitcast_fusion
  8.5 77.3 %all-reduce.6.cloned.1.call-done = f32[512,256]{1,0:T(8,128)} async-done(((f32[512,256]{1,0:T(8,128)}), f32[512,256]{1,0:T(8,128)}) %all-reduce.6.cloned.1.call-update) | async-done | bytes 524304 | tf_op jit(solution)/shard_map/psum | solution.py:11
  85.8 1.5 convolution_bitcast_fusion
  87.3 31.5 %all-gather = f32[512,256]{1,0:T(8,128)S(1)} all-gather(f32[64,256]{1,0:T(8,128)S(1)} %convolution_bitcast_fusion), channel_id=2, replica_groups=mesh['scen'=4,'col'=8] {'col'}, dimensions={0}, use_global_device_ids=true | all-gather | bytes 589824 | tf_op jit(solution)/shard_map/all_gather | solution.py:26
  118.8 7.3 %fusion.2 = f32[2048,256]{0,1:T(8,128)} fusion(f32[512,256]{1,0:T(8,128)S(1)} %all-gather, f32[1,512,2048]{2,1,0:T(8,128)} %param.3), kind=kOutput, calls=%fused_computation.4 | convolution fusion | flops 3221225472 | bytes 6815744 | tf_op jit(solution)/shard_map/skc,skp->cp/dot_general | solution.py:27
  126.1 1.7 fusion.18
  127.9 55.2 %all-reduce.8.cloned.1.call-done = (f32[2048,256]{0,1:T(8,128)}, f32[256,256]{0,1:T(8,128)}) async-done(((f32[2048,256]{0,1:T(8,128)}, f32[256,256]{0,1:T(8,128)}), (f32[2048,256]{0,1:T(8,128)}, f32[256,256]{0,1:T(8,128)})) %all-reduce.8.cloned.1.call-update) | async-done | bytes 2359312 | tf_op jit(solution)/shard_map/psum | solution.py:40
  183.1 1.0 select_add_fusion
  184.1 0.1 copy.5
  184.2 1.0 fusion.9
  185.2 0.1 copy.6
  185.4 11.7 %cholesky.49 = f32[128,128]{1,0:T(8,128)S(1)} custom-call(f32[128,128]{1,0:T(8,128)S(1)} %cholesky.115), custom_call_target="Cholesky" | custom-call | tf_op jit(solution)/shard_map/jit(cholesky)/cholesky | solution.py:46
  197.1 0.1 copy.7
  197.3 9.8 %custom-call.15 = f32[1,128,128]{1,2,0:T(8,128)S(1)} custom-call(f32[1,128,128]{2,1,0:T(8,128)S(1)} %get-tuple-element.32), custom_call_target="InvertDiagBlocksLowerTriangular" | custom-call | tf_op jit(solution)/shard_map/jit(cholesky)/cholesky | solution.py:46
  207.1 0.2 fusion.14
  207.4 0.3 convolution_subtract_fusion.1
  207.7 11.9 %cholesky.103 = f32[128,128]{1,0:T(8,128)S(1)} custom-call(f32[128,128]{1,0:T(8,128)S(1)} %convolution_subtract_fusion.1), custom_call_target="Cholesky" | custom-call | tf_op jit(solution)/shard_map/jit(cholesky)/cholesky | solution.py:46
  219.6 0.1 copy.9
  219.8 0.6 compare_reduce_fusion
  221.8 4.2 %while.1 = (s32[]{:T(128)}, f32[256,256]{0,1:T(8,128)S(1)}, s32[2,2]{1,0:T(2,128)S(1)}, f32[2,128,128]{2,1,0:T(8,128)S(1)}, s32[]{:T(128)}) while((s32[]{:T(128)}, f32[256,256]{0,1:T(8,128)S(1)}, s32[2,2]{1,0:T(2,128)S(1)}, f32[2,128,128]{2,1,0:T(8,128)S(1)}, s32[]{:T(128)}) %tuple.23), condition=%wide.while_cond, body=%wide.while_body.sunk | while | flops 2 | bytes 393329 | solution.py:47
  221.8 0.6 fusion.28
  222.4 1.4 dynamic-slice.7
  223.8 0.1 copy.15
  223.9 0.6 fusion.28
  224.5 1.4 dynamic-slice.7
  226.0 19.7 %custom-call.16 = f32[2,128,128]{1,2,0:T(8,128)S(1)} custom-call(f32[2,128,128]{2,1,0:T(8,128)S(1)} %get-tuple-element.12), custom_call_target="InvertDiagBlocksLowerTriangular" | custom-call | tf_op jit(solution)/shard_map/jit(_solve_triangular)/triangular_solve | solution.py:47
  245.7 0.3 add_bitcast_fusion
  246.0 1.0 fusion.6
  247.0 1.1 convolution_subtract_fusion
  248.1 1.1 fusion.13
  249.2 0.2 fusion.5
  249.4 1.8 copy.11
  (34 shorter events, 0.6 us)
Async XLA Ops:
  6.5 79.3 %copy-start = (f32[1,64,512]{2,1,0:T(8,128)S(1)}, f32[1,64,512]{2,1,0:T(8,128)}, u32[]{:S(2)}) copy-start(f32[1,64,512]{2,1,0:T(8,128)} %param.4) | copy-start | bytes 393220
  6.5 79.3 %all-reduce.6.cloned.1.call-start = ((), (), s32[]{:S(2)}) async-start(), calls=%async_computation | async-start | bytes 1048576 | tf_op jit(solution)/shard_map/psum | solution.py:11
  8.5 174.7 %all-reduce.8.cloned.1.call-start = ((), (), s32[]{:S(2)}) async-start(), calls=%async_computation.1 | async-start | bytes 4718592 | tf_op jit(solution)/shard_map/psum | solution.py:40
  118.8 7.3 %copy-start.2 = (f32[512,256]{1,0:T(8,128)S(1)}, f32[512,256]{1,0:T(8,128)}, u32[]{:S(2)}) copy-start(f32[512,256]{1,0:T(8,128)} %all-reduce.6.cloned.1.call-done) | copy-start | bytes 1572868
  126.1 1.8 copy-start.3
  207.3 38.4 %copy-start.1 = (f32[2048,256]{0,1:T(8,128)S(1)}, f32[2048,256]{0,1:T(8,128)}, u32[]{:S(2)}) copy-start(f32[2048,256]{0,1:T(8,128)} %get-tuple-element.25) | copy-start | bytes 6291460
  207.3 38.4 %dynamic-slice-start = ((f32[16384]{0:T(1024)}, s32[]{:T(128)}), f32[2048]{0:T(1024)S(1)}, s32[]{:S(2)}) async-start(f32[16384]{0:T(1024)} %param.5, s32[]{:T(128)} %select_n.32), calls=%async_computation.2 | async-start | bytes 16896 | tf_op jit(solution)/shard_map/dynamic_slice | solution.py:39
Sparse Core Ops, SparseCore 0:
  10.8 75.0 all-reduce.5
  128.0 55.1 all-reduce.7
where the time goes:
time: 258 us
  waiting for transfers between devices  133 us (52%)
  other arithmetic  58.2 us (23%)
  blocking collectives  31.5 us (12%)
  between operations  14.9 us (6%)
  matrix products  14.1 us (5%)
  local copies, waits for them, and re-layouts  6.58 us (3%)
    psum x1, waiting for transfers between devices, spread(): return lax.psum(kept, axis)  77.3 us
    psum x1, waiting for transfers between devices, shards(): summed, pivot_sum = lax.psum((running, pivot_run), 'scen')  55.2 us
    another operation x6, other arithmetic, shards(): factor = jnp.linalg.cholesky(pivot_matrix)  34.1 us
    all_gather x1, blocking collectives, shards(): block_piece = lax.all_gather(own_rows, 'col', axis=1, tiled=True)  31.5 us
    another operation x3, other arithmetic, shards(): jax.scipy.linalg.solve_triangular(factor, schur_rows.T, lower=True)  19.7 us
    dot_general x1, matrix products, shards(): jnp.einsum('skc,skp->cp', coupling, block_piece, precision=highest, prefe...  7.26 us
  transfers between devices with their start and end apart: 2, of which 2 were waited for; matrix products, arithmetic and copies ran while one was open for 0% of the time, Pallas kernels for 0%

commit v1 on v0

v1 whole, which is shorter than its diff:
```python
import functools

import jax
import jax.numpy as jnp
from jax import lax
from jax.experimental import pallas as pl
from jax.experimental.pallas import tpu as pltpu
from jax.sharding import PartitionSpec as P

PANEL = 256
HALF = PANEL // 2
QUEUE = 8
MESH = pl.DeviceIdType.MESH
HI = lax.Precision.HIGHEST
F32 = jnp.float32
BF16 = jnp.bfloat16


def split(value):
    high = value.astype(BF16)
    return high, (value - high.astype(F32)).astype(BF16)


def dot(a, b):
    return jnp.dot(a, b, preferred_element_type=F32)


def full(a, b, dims=((1,), (0,))):
    return lax.dot_general(a, b, (dims, ((), ())), precision=HI, preferred_element_type=F32)


def factor_block(a, step=2):
    size = a.shape[0]
    row = lax.broadcasted_iota(jnp.int32, (size, size), 0)
    col = lax.broadcasted_iota(jnp.int32, (size, size), 1)
    left, right = a, jnp.where(row == col, 1.0, 0.0).astype(F32)
    for k in range(0, size, step):
        base = k // 8 * 8
        l_live, r_live = left[base:], right[base:]
        rows = lax.broadcasted_iota(jnp.int32, (size - base, 1), 0) + base
        cols = [
            jnp.broadcast_to(l_live[:, k + t : k + t + 1], (size - base, size)) for t in range(step)
        ]
        lrows = [l_live[k + t - base : k + t + 1 - base] for t in range(step)]
        rrows = [r_live[k + t - base : k + t + 1 - base] for t in range(step)]
        for t in range(step):
            at = k + t - base
            inv = 1.0 / cols[t][at : at + 1]
            fac = jnp.where(rows > k + t, cols[t] * inv, 0.0)
            for u in range(t + 1, step):
                au = k + u - base
                cols[u] = cols[u] - fac * cols[u][at : at + 1]
                lrows[u] = lrows[u] - fac[au : au + 1] * lrows[t]
                rrows[u] = rrows[u] - fac[au : au + 1] * rrows[t]
            l_live = l_live - fac * lrows[t]
            r_live = r_live - fac * rrows[t]
        if base:
            left = jnp.concatenate([left[:base], l_live], axis=0)
            right = jnp.concatenate([right[:base], r_live], axis=0)
        else:
            left, right = l_live, r_live
    diag = jnp.sum(jnp.where(row == col, left, 0.0), axis=1, keepdims=True)
    scale = 1.0 / jnp.sqrt(diag)
    return jnp.where(row <= col, left * scale, 0.0), right * scale


def kernel(
    n_scen, n_col, pieces, c_ref, h_ref, d_ref, out_ref,
    cbuf, hbuf, pbuf, chi, clo, sendbuf, acc, crecv, xrecv, xout,
    piv, pivc, pivb, pivx,
    lsem, hsend, hrecv, psend, precv, csend, crsem, xsend, xrsem, osend, orsem, vsend, vrecv,
):
    scen, col = lax.axis_index("scen"), lax.axis_index("col")
    depth, n = cbuf.shape
    share = h_ref.shape[1]
    half = n // 2
    rows = half // pieces
    core = lax.rem(scen, 2)
    col_bits = [1 << i for i in reversed(range((n_col - 1).bit_length()))]
    scen_bits = [1 << i for i in range((n_scen - 1).bit_length())]

    def flip(index, bit):
        return jnp.where(lax.rem(index // bit, 2) == 0, index + bit, index - bit)

    def xor(index, mask):
        for b in col_bits:
            if mask & b:
                index = flip(index, b)
        return index

    def remote(src, dst, send, recv, who):
        return pltpu.make_async_remote_copy(
            src_ref=src, dst_ref=dst, send_sem=send, recv_sem=recv, device_id=who, device_id_type=MESH
        )

    load_c = pltpu.make_async_copy(c_ref.at[0], cbuf, lsem.at[0])
    load_c.start()
    load_h = pltpu.make_async_copy(
        h_ref.at[0], hbuf.at[pl.ds(pl.multiple_of(col * share, share), share)], lsem.at[1]
    )
    load_h.start()

    barrier = pltpu.get_barrier_semaphore()
    peers = [(scen, flip(col, b)) for b in col_bits]
    peers += [(scen, lax.rem(col + 2, n_col)), (scen, lax.rem(col + n_col - 2, n_col))]
    peers += [(flip(scen, b), col) for b in scen_bits]
    for peer in peers:
        pl.semaphore_signal(barrier, inc=1, device_id=peer, device_id_type=MESH)
    pl.semaphore_wait(barrier, len(peers))

    h_copies = []

    def h_send(d):
        owner = xor(col, d)
        where = hbuf.at[pl.ds(pl.multiple_of(owner * share, share), share)]
        for b in col_bits:
            if d == 0 or b < (d & -d):
                copy = remote(where, where, hsend.at[len(h_copies)], hrecv.at[d | b], (scen, flip(col, b)))
                copy.start()
                h_copies.append(copy)

    def h_wait(d):
        owner = xor(col, d)
        where = hbuf.at[pl.ds(pl.multiple_of(owner * share, share), share)]
        remote(where, where, hsend.at[0], hrecv.at[d], (scen, flip(col, 1))).wait_recv()

    even = lax.rem(col, 2) == 0
    along = jnp.logical_and(even, col + 2 < n_col)
    prow = depth // QUEUE

    def p_copy(q, which):
        where = pbuf.at[pl.ds(q * prow, prow)]
        target = lax.rem(col + 2, n_col) if which == 0 else flip(col, 1)
        return remote(where, where, psend.at[q, which], precv.at[q], (scen, target))

    def p_send(q):
        @pl.when(along)
        def _():
            p_copy(q, 0).start()

        @pl.when(even)
        def _():
            p_copy(q, 1).start()

    load_h.wait()
    h_send(0)
    load_c.wait()

    @pl.when(col == 0)
    def _():
        pbuf[...] = cbuf[:, :PANEL]

    blocks = n // 128
    order = sorted(range(1, n_col), key=lambda d: (bin(d).count("1"), -d))
    total = max(len(order), QUEUE)
    done = 0
    for i in range(total):
        for q in range(i * QUEUE // total, (i + 1) * QUEUE // total):
            @pl.when(col != 0)
            def _(q=q):
                p_copy(q, 1).wait_recv()
            p_send(q)
        for at in range(i * len(order) // total, (i + 1) * len(order) // total):
            h_wait(order[at])
            h_send(order[at])
        for j in range(i * blocks // total, (i + 1) * blocks // total):
            high, low = split(cbuf[:, j * 128 : (j + 1) * 128].T)
            chi[j * 128 : (j + 1) * 128] = high
            clo[j * 128 : (j + 1) * 128] = low

    panel = pbuf[...]
    solved = full(hbuf[...], panel)
    s_hi, s_lo = split(solved)
    panel_t = panel.T
    top = full(panel_t[:HALF], solved)
    piv[0:HALF] = top[:, :HALF]
    piv[HALF : 2 * HALF] = top[:, HALF:]
    piv[2 * HALF : 3 * HALF] = full(panel_t[HALF:], solved[:, HALF:])
    vrows = 3 * HALF // 2
    mine = pl.multiple_of(core * vrows, vrows)
    theirs = pl.multiple_of((1 - core) * vrows, vrows)
    pair = (flip(scen, 1), col)
    v0 = remote(piv.at[pl.ds(theirs, vrows)], pivc, vsend.at[0], vrecv.at[0], pair)
    v0.start()

    def term(start):
        start = pl.multiple_of(start, rows)
        high, low = chi[pl.ds(start, rows)], clo[pl.ds(start, rows)]
        return dot(high, s_hi) + (dot(high, s_lo) + dot(low, s_hi))

    c_copies = []
    for p in range(pieces):
        sendbuf[p] = term((1 - core) * half + p * rows)
        copy = remote(sendbuf.at[p], crecv.at[p], csend.at[p], crsem.at[p], pair)
        copy.start()
        c_copies.append(copy)

    def v_copy(i, bit):
        return remote(
            piv.at[pl.ds(mine, vrows)], pivx.at[i], vsend.at[i + 1], vrecv.at[i + 1], (flip(scen, bit), col)
        )

    v0.wait()
    piv[pl.ds(mine, vrows)] = piv[pl.ds(mine, vrows)] + pivc[...]
    stages = scen_bits[1:]
    v_copies = [v_copy(i, b) for i, b in enumerate(stages)]
    if v_copies:
        v_copies[0].start()

    def x_copy(i, p):
        return remote(
            acc.at[p], xrecv.at[i, p], xsend.at[i, p], xrsem.at[i, p], (flip(scen, stages[i]), col)
        )

    for p in range(pieces):
        own = term(core * half + p * rows)
        c_copies[p].wait()
        acc[p] = own + crecv[p]
        if stages:
            x_copy(0, p).start()
    for i in range(len(stages)):
        v_copies[i].wait()
        piv[pl.ds(mine, vrows)] = piv[pl.ds(mine, vrows)] + pivx[i]
        if i + 1 < len(stages):
            v_copies[i + 1].start()
    vback = remote(
        piv.at[pl.ds(mine, vrows)], pivb, vsend.at[len(stages) + 1], vrecv.at[len(stages) + 1], pair
    )
    vback.start()
    for i in range(len(stages) - 1):
        for p in range(pieces):
            x_copy(i, p).wait()
            acc[p] = acc[p] + xrecv[i, p]
            x_copy(i + 1, p).start()
    vback.wait()
    piv[pl.ds(theirs, vrows)] = pivb[...]

    eye = lax.broadcasted_iota(jnp.int32, (HALF, HALF), 0) == lax.broadcasted_iota(
        jnp.int32, (HALF, HALF), 1
    )
    a00 = piv[0:HALF]
    a01 = piv[HALF : 2 * HALF]
    a11 = piv[2 * HALF : 3 * HALF]
    a00 = 0.5 * (a00 + a00.T) + jnp.where(eye, d_ref[0:1, :], 0.0)
    a11 = 0.5 * (a11 + a11.T) + jnp.where(eye, d_ref[1:2, :], 0.0)
    u00, inv0 = factor_block(a00)
    u01 = full(inv0, a01)
    l10 = u01.T
    u11, inv1 = factor_block(a11 - full(l10, u01))
    inv10 = -full(inv1, full(l10, inv0))
    zero = jnp.zeros((HALF, HALF), F32)
    inverse = jnp.concatenate(
        [jnp.concatenate([inv0, zero], axis=1), jnp.concatenate([inv10, inv1], axis=1)], axis=0
    )

    o_copies = []
    last = len(stages) - 1
    for p in range(pieces):
        value = acc[p]
        if stages:
            x_copy(last, p).wait()
            value = value + xrecv[last, p]
        start = pl.multiple_of(core * half + p * rows, rows)
        xout[pl.ds(start, rows)] = full(value, inverse, ((1,), (1,)))
        copy = remote(xout.at[pl.ds(start, rows)], xout.at[pl.ds(start, rows)], osend.at[p], orsem.at[p], pair)
        copy.start()
        o_copies.append(copy)
    for p in range(pieces):
        o_copies[p].wait_send()
        start = pl.multiple_of((1 - core) * half + p * rows, rows)
        remote(xout.at[pl.ds(start, rows)], xout.at[pl.ds(start, rows)], osend.at[p], orsem.at[p], pair).wait_recv()

    @pl.when(col == 0)
    def _():
        xout[0:HALF, 0:HALF] = u00.T
        xout[0:HALF, HALF:] = zero
        xout[HALF:PANEL, 0:HALF] = l10
        xout[HALF:PANEL, HALF:] = u11.T

    store = pltpu.make_async_copy(xout, out_ref, lsem.at[2])
    store.start()
    for copy in h_copies:
        copy.wait_send()
    for q in range(QUEUE):
        @pl.when(along)
        def _(q=q):
            p_copy(q, 0).wait_send()

        @pl.when(even)
        def _(q=q):
            p_copy(q, 1).wait_send()
    store.wait()


def shards(n_scen, n_col, coupling, inverse_slabs, barrier_diagonal):
    depth, n = coupling.shape[1:]
    pieces = 4
    half = n // 2
    rows = half // pieces
    stages = max((n_scen - 1).bit_length() - 1, 1)
    dma = pltpu.SemaphoreType.DMA
    return pl.pallas_call(
        functools.partial(kernel, n_scen, n_col, pieces),
        out_shape=jax.ShapeDtypeStruct((n, PANEL), F32),
        in_specs=[pl.BlockSpec(memory_space=pl.ANY)] * 2 + [pl.BlockSpec(memory_space=pltpu.VMEM)],
        out_specs=pl.BlockSpec(memory_space=pl.ANY),
        scratch_shapes=[
            pltpu.VMEM((depth, n), F32),
            pltpu.VMEM((depth, depth), F32),
            pltpu.VMEM((depth, PANEL), F32),
            pltpu.VMEM((n, depth), BF16),
            pltpu.VMEM((n, depth), BF16),
            pltpu.VMEM((pieces, rows, PANEL), F32),
            pltpu.VMEM((pieces, rows, PANEL), F32),
            pltpu.VMEM((pieces, rows, PANEL), F32),
            pltpu.VMEM((stages, pieces, rows, PANEL), F32),
            pltpu.VMEM((n, PANEL), F32),
            pltpu.VMEM((3 * HALF, HALF), F32),
            pltpu.VMEM((3 * HALF // 2, HALF), F32),
            pltpu.VMEM((3 * HALF // 2, HALF), F32),
            pltpu.VMEM((stages, 3 * HALF // 2, HALF), F32),
            dma((3,)),
            dma((n_col,)),
            dma((n_col,)),
            dma((QUEUE, 2)),
            dma((QUEUE,)),
            dma((pieces,)),
            dma((pieces,)),
            dma((stages, pieces)),
            dma((stages, pieces)),
            dma((pieces,)),
            dma((pieces,)),
            dma((stages + 2,)),
            dma((stages + 2,)),
        ],
        compiler_params=pltpu.CompilerParams(
            collective_id=0, has_side_effects=True, vmem_limit_bytes=40 * 1024 * 1024
        ),
    )(coupling, inverse_slabs, barrier_diagonal.reshape(-1, 128))


def solution(mesh):
    return jax.shard_map(
        functools.partial(shards, mesh.shape["scen"], mesh.shape["col"]),
        mesh=mesh,
        in_specs=(P("scen", None, "col"), P("scen", "col", None), P(None)),
        out_specs=P("col", None),
        check_vma=False,
    )
```

time: 258 us -> 78.1 us (0.30)
  the two profiles are of different devices: /device:TPU:0 before, /device:TPU:25 now
where the time goes in v1:
time: 78.1 us; the launch traced here: 77.9 us
  Pallas kernels  72.6 us (93%)
  local copies, waits for them, and re-layouts  5.25 us (7%)
    pallas_call x1, Pallas kernels, shards(): pl.pallas_call(functools.partial(kernel, n_scen, n_col, pieces), out_shap...  72.6 us
    unnamed x7, local copies, waits for them, and re-layouts  5.25 us

profile of v1, /device:TPU:25, one launch (start us, length us, event | category | flops | bytes accessed | tf_op | source)
XLA Modules:
  0.0 77.9 jit_solution(8561801875928662659)
XLA Ops:
  0.0 0.0 copy-start
  0.0 2.2 %copy-done = f32[1,512,2048]{2,1,0:T(8,128)S(1)} copy-done((f32[1,512,2048]{2,1,0:T(8,128)S(1)}, f32[1,512,2048]{2,1,0:T(8,128)}, u32[]{:S(2)}) %copy-start) | copy-done | bytes 4194328
  2.2 0.0 copy-start.1
  2.2 0.9 %copy-done.1 = f32[1,64,512]{2,1,0:T(8,128)S(1)} copy-done((f32[1,64,512]{2,1,0:T(8,128)S(1)}, f32[1,64,512]{2,1,0:T(8,128)}, u32[]{:S(2)}) %copy-start.1) | copy-done | bytes 131096
  3.1 0.0 copy-start.2
  3.1 0.8 %copy-done.2 = f32[16384]{0:T(1024)S(1)} copy-done((f32[16384]{0:T(1024)S(1)}, f32[16384]{0:T(1024)}, u32[]{:S(2)}) %copy-start.2) | copy-done | bytes 65560
  3.9 72.6 %shard_map.37 = f32[2048,256]{1,0:T(8,128)S(1)} custom-call(f32[1,512,2048]{2,1,0:T(8,128)S(1)} %copy-done, f32[1,64,512]{2,1,0:T(8,128)S(1)} %copy-done.1, f32[128,128]{1,0:T(8,128)S(1)} %bitcast.1), custom_call_target="tpu_custom_call" | custom-call | tf_op jit(solution)/shard_map/pallas_call | solution.py:302
  76.6 1.3 %copy.5 = f32[2048,256]{1,0:T(8,128)} copy(f32[2048,256]{1,0:T(8,128)S(1)} %shard_map.37) | data formatting | bytes 4194304
Async XLA Ops:
  0.0 2.2 %copy-start = (f32[1,512,2048]{2,1,0:T(8,128)S(1)}, f32[1,512,2048]{2,1,0:T(8,128)}, u32[]{:S(2)}) copy-start(f32[1,512,2048]{2,1,0:T(8,128)} %c_ref.1) | copy-start | bytes 12582916
  2.2 0.9 %copy-start.1 = (f32[1,64,512]{2,1,0:T(8,128)S(1)}, f32[1,64,512]{2,1,0:T(8,128)}, u32[]{:S(2)}) copy-start(f32[1,64,512]{2,1,0:T(8,128)} %h_ref.1) | copy-start | bytes 393220
  3.1 0.8 %copy-start.2 = (f32[16384]{0:T(1024)S(1)}, f32[16384]{0:T(1024)}, u32[]{:S(2)}) copy-start(f32[16384]{0:T(1024)} %param.5) | copy-start | bytes 196612

commit v2 on v1

--- a/solution.py
+++ b/solution.py
@@ -66,9 +66,9 @@
 
 def kernel(
     n_scen, n_col, pieces, c_ref, h_ref, d_ref, out_ref,
-    cbuf, hbuf, pbuf, chi, clo, sendbuf, acc, crecv, xrecv, xout,
+    cbuf, dbuf, hbuf, pbuf, sbuf, chi, clo, sendbuf, acc, crecv, xrecv, xout,
     piv, pivc, pivb, pivx,
-    lsem, hsend, hrecv, psend, precv, csend, crsem, xsend, xrsem, osend, orsem, vsend, vrecv,
+    lsem, ssend, srecv, psend, precv, csend, crsem, xsend, xrsem, osend, orsem, vsend, vrecv,
 ):
     scen, col = lax.axis_index("scen"), lax.axis_index("col")
     depth, n = cbuf.shape
@@ -94,11 +94,20 @@
         )
 
     load_c = pltpu.make_async_copy(c_ref.at[0], cbuf, lsem.at[0])
+    load_d = pltpu.make_async_copy(d_ref.at[pl.ds(0, 8)], dbuf, lsem.at[3])
+    load_h = pltpu.make_async_copy(h_ref.at[0], hbuf, lsem.at[1])
+
+    def load_p(t):
+        return pltpu.make_async_copy(c_ref.at[0, :, pl.ds(t * HALF, HALF)], pbuf.at[t], lsem.at[4 + t])
+
+    @pl.when(col == 0)
+    def _():
+        load_p(0).start()
+        load_p(1).start()
+
+    load_h.start()
     load_c.start()
-    load_h = pltpu.make_async_copy(
-        h_ref.at[0], hbuf.at[pl.ds(pl.multiple_of(col * share, share), share)], lsem.at[1]
-    )
-    load_h.start()
+    load_d.start()
 
     barrier = pltpu.get_barrier_semaphore()
     peers = [(scen, flip(col, b)) for b in col_bits]
@@ -108,70 +117,113 @@
         pl.semaphore_signal(barrier, inc=1, device_id=peer, device_id_type=MESH)
     pl.semaphore_wait(barrier, len(peers))
 
-    h_copies = []
-
-    def h_send(d):
+    s_copies = []
+
+    def s_send(d):
         owner = xor(col, d)
-        where = hbuf.at[pl.ds(pl.multiple_of(owner * share, share), share)]
+        where = sbuf.at[pl.ds(pl.multiple_of(owner * share, share), share)]
         for b in col_bits:
             if d == 0 or b < (d & -d):
-                copy = remote(where, where, hsend.at[len(h_copies)], hrecv.at[d | b], (scen, flip(col, b)))
+                copy = remote(where, where, ssend.at[len(s_copies)], srecv.at[d | b], (scen, flip(col, b)))
                 copy.start()
-                h_copies.append(copy)
-
-    def h_wait(d):
+                s_copies.append(copy)
+
+    def s_wait(d):
         owner = xor(col, d)
-        where = hbuf.at[pl.ds(pl.multiple_of(owner * share, share), share)]
-        remote(where, where, hsend.at[0], hrecv.at[d], (scen, flip(col, 1))).wait_recv()
-
-    even = lax.rem(col, 2) == 0
-    along = jnp.logical_and(even, col + 2 < n_col)
+        where = sbuf.at[pl.ds(pl.multiple_of(owner * share, share), share)]
+        remote(where, where, ssend.at[0], srecv.at[d], (scen, flip(col, 1))).wait_recv()
+
+    side, pair_at = lax.rem(col, 2), col // 2
     prow = depth // QUEUE
-
-    def p_copy(q, which):
-        where = pbuf.at[pl.ds(q * prow, prow)]
-        target = lax.rem(col + 2, n_col) if which == 0 else flip(col, 1)
-        return remote(where, where, psend.at[q, which], precv.at[q], (scen, target))
-
-    def p_send(q):
-        @pl.when(along)
-        def _():
-            p_copy(q, 0).start()
-
-        @pl.when(even)
-        def _():
-            p_copy(q, 1).start()
-
-    load_h.wait()
-    h_send(0)
-    load_c.wait()
+    ahead = pair_at + 1 < n_col // 2
+    across = pair_at >= 1
+    returns = col == 3
+
+    def p_copy(t, q, slot, target):
+        where = pbuf.at[t, pl.ds(q * prow, prow)]
+        return remote(where, where, psend.at[slot, q], precv.at[t, q], (scen, target))
+
+    def p_wait(t, q):
+        p_copy(t, q, 0, flip(col, 1)).wait_recv()
+
+    def p_ahead(q):
+        return p_copy(side, q, 0, lax.rem(col + 2, n_col))
+
+    def p_across(q):
+        return p_copy(side, q, 1, flip(col, 1))
+
+    def p_first(q):
+        return p_copy(1, q, 1, flip(col, 1))
+
+    def p_back(q):
+        return p_copy(0, q, 2, lax.rem(col + n_col - 2, n_col))
+
+    def transpose(j):
+        high, low = split(cbuf[:, j * 128 : (j + 1) * 128].T)
+        chi[j * 128 : (j + 1) * 128] = high
+        clo[j * 128 : (j + 1) * 128] = low
+
+    blocks = n // 128
+    early = blocks // 2
 
     @pl.when(col == 0)
     def _():
-        pbuf[...] = cbuf[:, :PANEL]
-
-    blocks = n // 128
+        load_p(0).wait()
+        load_p(1).wait()
+
+    for q in range(QUEUE):
+        @pl.when(col != 0)
+        def _(q=q):
+            p_wait(side, q)
+
+        @pl.when(ahead)
+        def _(q=q):
+            p_ahead(q).start()
+
+        @pl.when(across)
+        def _(q=q):
+            p_across(q).start()
+
+        @pl.when(col == 0)
+        def _(q=q):
+            p_first(q).start()
+
+        if q:
+            @pl.when(returns)
+            def _(q=q):
+                p_wait(0, q - 1)
+                p_back(q - 1).start()
+        if q == 0:
+            load_c.wait()
+        for j in range(q * early // QUEUE, (q + 1) * early // QUEUE):
+            transpose(j)
+
+    @pl.when(returns)
+    def _():
+        p_wait(0, QUEUE - 1)
+        p_back(QUEUE - 1).start()
+
+    @pl.when(jnp.logical_and(col != 0, col != 3))
+    def _():
+        for q in range(QUEUE):
+            p_wait(1 - side, q)
+
+    load_h.wait()
+    load_d.wait()
+    panel = jnp.concatenate([pbuf[0], pbuf[1]], axis=1)
+    sbuf[pl.ds(pl.multiple_of(col * share, share), share)] = full(hbuf[...], panel)
+    s_send(0)
+    panel_t = panel.T
     order = sorted(range(1, n_col), key=lambda d: (bin(d).count("1"), -d))
-    total = max(len(order), QUEUE)
-    done = 0
-    for i in range(total):
-        for q in range(i * QUEUE // total, (i + 1) * QUEUE // total):
-            @pl.when(col != 0)
-            def _(q=q):
-                p_copy(q, 1).wait_recv()
-            p_send(q)
-        for at in range(i * len(order) // total, (i + 1) * len(order) // total):
-            h_wait(order[at])
-            h_send(order[at])
-        for j in range(i * blocks // total, (i + 1) * blocks // total):
-            high, low = split(cbuf[:, j * 128 : (j + 1) * 128].T)
-            chi[j * 128 : (j + 1) * 128] = high
-            clo[j * 128 : (j + 1) * 128] = low
-
-    panel = pbuf[...]
-    solved = full(hbuf[...], panel)
+    for i, d in enumerate(order):
+        s_wait(d)
+        s_send(d)
+        late = blocks - early
+        for j in range(early + i * late // len(order), early + (i + 1) * late // len(order)):
+            transpose(j)
+
+    solved = sbuf[...]
     s_hi, s_lo = split(solved)
-    panel_t = panel.T
     top = full(panel_t[:HALF], solved)
     piv[0:HALF] = top[:, :HALF]
     piv[HALF : 2 * HALF] = top[:, HALF:]
@@ -241,8 +293,8 @@
     a00 = piv[0:HALF]
     a01 = piv[HALF : 2 * HALF]
     a11 = piv[2 * HALF : 3 * HALF]
-    a00 = 0.5 * (a00 + a00.T) + jnp.where(eye, d_ref[0:1, :], 0.0)
-    a11 = 0.5 * (a11 + a11.T) + jnp.where(eye, d_ref[1:2, :], 0.0)
+    a00 = 0.5 * (a00 + a00.T) + jnp.where(eye, dbuf[0:1, :], 0.0)
+    a11 = 0.5 * (a11 + a11.T) + jnp.where(eye, dbuf[1:2, :], 0.0)
     u00, inv0 = factor_block(a00)
     u01 = full(inv0, a01)
     l10 = u01.T
@@ -279,16 +331,24 @@
 
     store = pltpu.make_async_copy(xout, out_ref, lsem.at[2])
     store.start()
-    for copy in h_copies:
+    for copy in s_copies:
         copy.wait_send()
     for q in range(QUEUE):
-        @pl.when(along)
-        def _(q=q):
-            p_copy(q, 0).wait_send()
-
-        @pl.when(even)
-        def _(q=q):
-            p_copy(q, 1).wait_send()
+        @pl.when(ahead)
+        def _(q=q):
+            p_ahead(q).wait_send()
+
+        @pl.when(across)
+        def _(q=q):
+            p_across(q).wait_send()
+
+        @pl.when(col == 0)
+        def _(q=q):
+            p_first(q).wait_send()
+
+        @pl.when(returns)
+        def _(q=q):
+            p_back(q).wait_send()
     store.wait()
 
 
@@ -302,11 +362,13 @@
     return pl.pallas_call(
         functools.partial(kernel, n_scen, n_col, pieces),
         out_shape=jax.ShapeDtypeStruct((n, PANEL), F32),
-        in_specs=[pl.BlockSpec(memory_space=pl.ANY)] * 2 + [pl.BlockSpec(memory_space=pltpu.VMEM)],
+        in_specs=[pl.BlockSpec(memory_space=pltpu.HBM)] * 3,
         out_specs=pl.BlockSpec(memory_space=pl.ANY),
         scratch_shapes=[
             pltpu.VMEM((depth, n), F32),
-            pltpu.VMEM((depth, depth), F32),
+            pltpu.VMEM((8, 128), F32),
+            pltpu.VMEM((inverse_slabs.shape[1], depth), F32),
+            pltpu.VMEM((2, depth, HALF), F32),
             pltpu.VMEM((depth, PANEL), F32),
             pltpu.VMEM((n, depth), BF16),
             pltpu.VMEM((n, depth), BF16),
@@ -319,11 +381,11 @@
             pltpu.VMEM((3 * HALF // 2, HALF), F32),
             pltpu.VMEM((3 * HALF // 2, HALF), F32),
             pltpu.VMEM((stages, 3 * HALF // 2, HALF), F32),
-            dma((3,)),
+            dma((6,)),
             dma((n_col,)),
             dma((n_col,)),
-            dma((QUEUE, 2)),
-            dma((QUEUE,)),
+            dma((3, QUEUE)),
+            dma((2, QUEUE)),
             dma((pieces,)),
             dma((pieces,)),
             dma((stages, pieces)),

time: 78.1 us -> 73.4 us (0.940)
  the two profiles are of different devices: /device:TPU:25 before, /device:TPU:0 now
where the time goes in v2:
time: 73.4 us; the launch traced here: 72.1 us
  Pallas kernels  66.8 us (91%)
  local copies, waits for them, and re-layouts  5.25 us (7%)
    pallas_call x1, Pallas kernels, shards(): pl.pallas_call(functools.partial(kernel, n_scen, n_col, pieces), out_shap...  66.8 us
    unnamed x7, local copies, waits for them, and re-layouts  5.25 us

profile of v2, /device:TPU:0, one launch (start us, length us, event | category | flops | bytes accessed | tf_op | source)
XLA Modules:
  0.0 72.1 jit_solution(9589899266040276575)
XLA Ops:
  0.0 0.0 copy-start
  0.0 2.2 %copy-done = f32[1,512,2048]{2,1,0:T(8,128)S(1)} copy-done((f32[1,512,2048]{2,1,0:T(8,128)S(1)}, f32[1,512,2048]{2,1,0:T(8,128)}, u32[]{:S(2)}) %copy-start) | copy-done | bytes 4194328
  2.2 0.0 copy-start.1
  2.2 0.9 %copy-done.1 = f32[1,64,512]{2,1,0:T(8,128)S(1)} copy-done((f32[1,64,512]{2,1,0:T(8,128)S(1)}, f32[1,64,512]{2,1,0:T(8,128)}, u32[]{:S(2)}) %copy-start.1) | copy-done | bytes 131096
  3.1 0.0 copy-start.2
  3.1 0.8 %copy-done.2 = f32[16384]{0:T(1024)S(1)} copy-done((f32[16384]{0:T(1024)S(1)}, f32[16384]{0:T(1024)}, u32[]{:S(2)}) %copy-start.2) | copy-done | bytes 65560
  3.9 66.8 %shard_map.37 = f32[2048,256]{1,0:T(8,128)S(1)} custom-call(f32[1,512,2048]{2,1,0:T(8,128)S(1)} %copy-done, f32[1,64,512]{2,1,0:T(8,128)S(1)} %copy-done.1, f32[128,128]{1,0:T(8,128)S(1)} %bitcast.1), custom_call_target="tpu_custom_call" | custom-call | tf_op jit(solution)/shard_map/pallas_call | solution.py:362
  70.8 1.3 %copy.5 = f32[2048,256]{1,0:T(8,128)} copy(f32[2048,256]{1,0:T(8,128)S(1)} %shard_map.37) | data formatting | bytes 4194304
Async XLA Ops:
  0.0 2.2 %copy-start = (f32[1,512,2048]{2,1,0:T(8,128)S(1)}, f32[1,512,2048]{2,1,0:T(8,128)}, u32[]{:S(2)}) copy-start(f32[1,512,2048]{2,1,0:T(8,128)} %c_ref.1) | copy-start | bytes 12582916
  2.2 0.9 %copy-start.1 = (f32[1,64,512]{2,1,0:T(8,128)S(1)}, f32[1,64,512]{2,1,0:T(8,128)}, u32[]{:S(2)}) copy-start(f32[1,64,512]{2,1,0:T(8,128)} %h_ref.1) | copy-start | bytes 393220
  3.1 0.8 %copy-start.2 = (f32[16384]{0:T(1024)S(1)}, f32[16384]{0:T(1024)}, u32[]{:S(2)}) copy-start(f32[16384]{0:T(1024)} %param.5) | copy-start | bytes 196612
